TPU v7x, 512 devices: a whole 4x4x16 slice. The times are simulated.
512 devices in a mesh: ctx: 64 (over y, z), exp: 8 (over x, core).
Axes of the slice: x: 4, y: 4, z: 16, core: 2. Of those that a mesh axis runs over, the one named last changes fastest.
Arguments:
- x_resid: bfloat16 [512, 6144], P('exp', 'ctx'), may hold values from -16 to 16
- queries: bfloat16 [512, 6144], P('ctx', 'exp'), may hold values from -5 to 5
- keys: bfloat16 [32768, 1024], P('ctx', 'exp'), may hold values from -4 to 4
- values: bfloat16 [32768, 1024], P('ctx', 'exp'), may hold values from -4 to 4
- pattern: int32 [4, 6], replicated, may hold values from 0 to 254, as said below
- global_blocks: int32 [2], replicated, may hold values from 0 to 248, as said below
- out_weight: bfloat16 [6144, 6144], P('exp', 'ctx'), may hold values from -0.875 to 0.875
- norm_gain: float32 [6144], P('ctx'), may hold values from 0.1 to 1.9
- router: bfloat16 [6144, 8], P('ctx'), may hold values from -0.078125 to 0.078125
- expert_ids: int32 [512, 2], P('exp'), may hold values from 0 to 7, as said below
- expert_slots: int32 [512, 2], P('exp'), may hold values from 0 to 19, as said below
- w_gate: bfloat16 [8, 6144, 8192], P('exp', None, 'ctx'), may hold values from -0.078125 to 0.078125
- w_up: bfloat16 [8, 6144, 8192], P('exp', None, 'ctx'), may hold values from -0.078125 to 0.078125
- w_down: bfloat16 [8, 8192, 6144], P('exp', None, 'ctx'), may hold values from -0.0625 to 0.0625
Outputs:
- layer_out: bfloat16 [512, 6144], P('exp', 'ctx')
Inputs may be any that keep to these rules, and one draw needn't show every extreme that they name: `pattern`: each row lists 3 + 3 different key blocks, none of them a global block. `global_blocks`: 2 different key blocks. `expert_ids`: each token names two different experts; among the tokens of one index of exp (aligned blocks of 64 rows) every expert is named at most 20 times, and one expert, the same in every block, exactly 20 times. `expert_slots`: within one aligned block of 64 rows, the choices that name the same expert have different slots.
All inputs are finite; a program needn't handle non-finite values.
Results may differ from a plain program's by a relative error of at most 0.01.
Values may be sent and summed in bfloat16 or wider, within the bound.
No kernel may reach another device: no remote copies, remote signals or barrier semaphores. Data moves between devices by JAX's collectives and lax.ppermute only.
A program may use at most 64 MiB of HBM per device.

v0:
```python
import jax
import jax.numpy as jnp
from jax import lax
from jax.sharding import PartitionSpec as P

D = 6144
HD = 128
BLK = 128
CAP = 20
eps = 1e-05
masked_score = -1e30


def per_device(
    x_resid,
    queries,
    keys,
    values,
    pattern,
    global_blocks,
    out_weight,
    norm_gain,
    router,
    expert_ids,
    expert_slots,
    w_gate,
    w_up,
    w_down,
):
    all_queries = lax.all_gather(queries, "ctx", axis=0, tiled=True)
    token_count = all_queries.shape[0]
    cache_length = keys.shape[0]
    groups_local = keys.shape[1] // HD
    group = all_queries.shape[1] // HD // groups_local
    query_heads = all_queries.reshape(token_count, groups_local, group, HD)
    key_heads = keys.reshape(cache_length, groups_local, HD)
    value_heads = values.reshape(cache_length, groups_local, HD)
    scores = jnp.einsum(
        "tkgd,pkd->tkgp", query_heads, key_heads, preferred_element_type=jnp.float32
    ) * HD ** (-0.5)
    local_blocks = cache_length // BLK
    block_ids = lax.axis_index("ctx") * local_blocks + jnp.arange(local_blocks, dtype=jnp.int32)
    listed = jnp.any(pattern[:, :, None] == block_ids[None, None, :], axis=1)
    anchored = jnp.any(global_blocks[:, None] == block_ids[None, :], axis=0)
    allowed_blocks = listed | anchored[None, :]
    allowed = jnp.repeat(jnp.repeat(allowed_blocks, BLK, axis=0), BLK, axis=1)[:, None, None, :]
    local_peak = jnp.max(jnp.where(allowed, scores, masked_score), axis=-1)
    peak = lax.pmax(local_peak, "ctx")
    probs = jnp.where(allowed, jnp.exp(scores - peak[..., None]), 0.0).astype(jnp.bfloat16)
    numerator = jnp.einsum("tkgp,pkd->tkgd", probs, value_heads, preferred_element_type=jnp.float32)
    denominator = jnp.sum(probs, axis=-1, dtype=jnp.float32)
    numerator, denominator = lax.psum((numerator, denominator), "ctx")
    attention = (numerator / denominator[..., None]).astype(jnp.bfloat16).reshape(token_count, -1)
    exp_count = lax.axis_size("exp")
    head_total = lax.psum_scatter(
        jnp.dot(attention, out_weight, preferred_element_type=jnp.float32),
        "exp",
        scatter_dimension=0,
        tiled=True,
    )
    residual = x_resid.astype(jnp.float32) + head_total
    scaled = residual * norm_gain
    router_wide = router.astype(jnp.float32)
    squares = lax.psum(jnp.sum(residual * residual, axis=1), "ctx")
    inverse = lax.rsqrt(squares / D + eps)
    logits = lax.psum(
        jnp.dot(scaled * inverse[:, None], router_wide, precision=lax.Precision.HIGHEST), "ctx"
    )
    normed = (scaled * inverse[:, None]).astype(jnp.bfloat16)
    experts_all = router.shape[1]
    onehot = expert_ids[:, :, None] == jnp.arange(experts_all, dtype=jnp.int32)[None, None, :]
    chosen_logits = jnp.sum(jnp.where(onehot, logits[:, None, :], 0.0), axis=-1)
    gate_weights = jax.nn.sigmoid(chosen_logits - chosen_logits[:, ::-1])
    flat_slots = expert_ids * CAP + expert_slots
    positions = jnp.arange(experts_all * CAP, dtype=jnp.int32)
    dispatch = jnp.sum(
        (flat_slots[None, :, :] == positions[:, None, None]).astype(jnp.bfloat16), axis=2
    )
    local_experts = w_gate.shape[0]
    feature_rows = lax.all_gather(normed, "ctx", axis=1, tiled=True)
    outgoing = jnp.dot(dispatch, feature_rows, preferred_element_type=jnp.float32).astype(
        jnp.bfloat16
    )
    outgoing = outgoing.reshape(experts_all, CAP, -1)
    incoming = lax.all_to_all(outgoing, "exp", split_axis=0, concat_axis=0, tiled=True)
    incoming = incoming.reshape(exp_count, local_experts, CAP, -1)
    expert_gate = jnp.einsum("sjcd,jdf->sjcf", incoming, w_gate, preferred_element_type=jnp.float32)
    expert_lift = jnp.einsum("sjcd,jdf->sjcf", incoming, w_up, preferred_element_type=jnp.float32)
    hidden = (jax.nn.silu(expert_gate) * expert_lift).astype(jnp.bfloat16)
    out_width = w_down.shape[2]
    expert_out = jnp.einsum(
        "sjcf,jfd->sjcd",
        lax.all_gather(hidden, "ctx", axis=3, tiled=True),
        w_down,
        preferred_element_type=jnp.float32,
    ).astype(jnp.bfloat16)
    returned = lax.all_to_all(
        expert_out.reshape(experts_all, CAP, out_width),
        "exp",
        split_axis=0,
        concat_axis=0,
        tiled=True,
    )
    picked = jnp.take(returned.reshape(experts_all * CAP, out_width), flat_slots, axis=0).astype(
        jnp.float32
    )
    mixture = jnp.sum(gate_weights[:, :, None] * picked, axis=1)
    return (residual + mixture).astype(jnp.bfloat16)


def solution(mesh):
    in_specs = (
        P("exp", "ctx"),
        P("ctx", "exp"),
        P("ctx", "exp"),
        P("ctx", "exp"),
        P(),
        P(),
        P("exp", "ctx"),
        P("ctx"),
        P("ctx", None),
        P("exp", None),
        P("exp", None),
        P("exp", None, "ctx"),
        P("exp", None, "ctx"),
        P("exp", None, "ctx"),
    )
    out_specs = P("exp", "ctx")
    return jax.shard_map(
        per_device, mesh=mesh, in_specs=in_specs, out_specs=out_specs, check_vma=False
    )
```

profile of v0, /device:TPU:1, one launch (start us, length us, event | category | flops | bytes accessed | tf_op | source)
XLA Modules:
  0.0 1161.9 jit_solution(5624072325766790315)
XLA Ops:
  6.5 0.0 copy-start
  6.5 0.0 all-reduce.2.cloned.1.call-start
  6.5 1.0 compare_reduce_fusion
  7.6 0.8 compare_reduce_fusion.1
  8.3 0.1 copy.41
  8.4 0.1 broadcast_bitcast_fusion
  8.5 82.7 %all_gather.9 = bf16[512,768]{1,0:T(8,128)(2,1)S(1)} all-gather(bf16[8,768]{1,0:T(8,128)(2,1)} %param.15), channel_id=1, replica_groups=mesh['ctx'=64,'exp'=8] {'ctx'}, dimensions={0}, use_global_device_ids=true | all-gather | bytes 798720 | tf_op jit(solution)/shard_map/all_gather | solution.py:30
  91.3 0.3 copy.42
  91.5 0.1 broadcast_in_dim.67
  91.6 0.0 copy-start.16
  91.6 4.8 fusion
  96.4 221.4 %pmax.7 = f32[512,6]{0,1:T(8,128)S(1)} all-reduce(f32[512,6]{0,1:T(8,128)S(1)} %get-tuple-element.7), channel_id=1, replica_groups=mesh['ctx'=64,'exp'=8] {'ctx'}, use_global_device_ids=true, to_apply=%region_3.4 | all-reduce | flops 3072 | bytes 24576 | tf_op jit(solution)/shard_map/pmax | solution.py:48
  317.8 0.0 copy-done.16
  317.8 5.6 fusion.13
  323.4 0.0 all-reduce.2.cloned.1.call-update
  323.4 0.0 reduce-scatter.2.cloned.1.call-start
  323.5 4.1 convert_reduce_fusion
  327.6 0.0 copy-start.4
  327.6 0.0 copy-start.8
  327.6 0.0 copy-start.11
  327.6 0.0 copy-start.5
  327.6 0.0 copy-start.12
  327.6 219.7 %psum.29 = f32[512,6]{0,1:T(8,128)S(1)} all-reduce(f32[512,6]{0,1:T(8,128)S(1)} %convert_reduce_fusion), channel_id=1, replica_groups=mesh['ctx'=64,'exp'=8] {'ctx'}, use_global_device_ids=true, to_apply=%region_6.7 | all-reduce | flops 3072 | bytes 24576 | tf_op jit(solution)/shard_map/psum | solution.py:52
  547.3 113.2 %all-reduce.2.cloned.1.call-done = f32[512,1,6,128]{3,0,2,1:T(8,128)} async-done(((f32[512,1,6,128]{3,0,2,1:T(8,128)}), f32[512,1,6,128]{3,0,2,1:T(8,128)}) %all-reduce.2.cloned.1.call-update) | async-done | bytes 1572880 | tf_op jit(solution)/shard_map/psum | solution.py:52
  660.5 1.9 divide_convert_fusion
  662.4 0.3 copy.45
  662.7 1.1 fusion.44
  663.8 0.0 reduce-scatter.2.cloned.1.call-update
  663.8 0.0 all-gather.3.cloned.1.call-start
  663.9 0.0 copy-done.8
  663.9 0.0 copy-done.11
  663.9 0.6 compare_and_fusion
  664.5 0.6 copy-done.6
  665.0 0.7 fusion.37
  665.7 45.5 %reduce-scatter.2.cloned.1.call-done = f32[64,96]{1,0:T(8,128)} async-done(((f32[512,96]{1,0:T(8,128)}), f32[64,96]{1,0:T(8,128)}) %reduce-scatter.2.cloned.1.call-update) | async-done | bytes 24592 | tf_op jit(solution)/shard_map/reduce_scatter | solution.py:55
  711.2 0.9 multiply_reduce_fusion.1
  712.1 115.6 %psum.30 = f32[64]{0:T(128)S(1)} all-reduce(f32[64]{0:T(128)S(1)} %multiply_reduce_fusion.1), channel_id=1, replica_groups=mesh['ctx'=64,'exp'=8] {'ctx'}, use_global_device_ids=true, to_apply=%region_9.10 | all-reduce | flops 64 | bytes 512 | tf_op jit(solution)/shard_map/psum | solution.py:64
  827.7 0.8 fusion.40
  828.5 72.3 %all-gather = bf16[64,96,64]{1,2,0:T(8,128)(2,1)S(1)} all-gather(bf16[1,96,64]{1,2,0:T(8,128)(2,1)S(1)} %fusion.40), channel_id=1, replica_groups=mesh['ctx'=64,'exp'=8] {'ctx'}, dimensions={0}, use_global_device_ids=true | all-gather | bytes 798720 | tf_op jit(solution)/shard_map/all_gather | solution.py:80
  900.8 0.7 copy.48
  901.5 2.3 reshape.108
  903.8 1.8 convolution_convert_fusion
  905.7 2.1 reshape.89
  907.8 88.6 %all_to_all.10 = bf16[8,20,6144]{2,1,0:T(8,128)(2,1)S(1)} all-to-all(bf16[8,20,6144]{2,1,0:T(8,128)(2,1)} %reshape.89), channel_id=1, replica_groups=mesh['ctx'=64,'exp'=8] {'exp'}, dimensions={0} | all-to-all | bytes 3932160 | tf_op jit(solution)/shard_map/all_to_all | solution.py:85
  996.4 0.0 copy-start.13
  996.5 0.0 copy-start.15
  996.5 0.0 copy-start.17
  996.5 0.8 fusion.16
  997.3 0.6 copy-done.1
  997.8 1.4 fusion.25
  999.2 0.0 all-gather.3.cloned.1.call-update
  999.3 0.1 copy.49
  999.4 0.1 reshape.99
  999.5 0.1 copy.47
  999.7 0.2 fusion.39
  999.9 113.2 %psum.31 = f32[64,8]{0,1:T(8,128)S(1)} all-reduce(f32[64,8]{0,1:T(8,128)S(1)} %fusion.39), channel_id=1, replica_groups=mesh['ctx'=64,'exp'=8] {'ctx'}, use_global_device_ids=true, to_apply=%region_10.11 | all-reduce | flops 512 | bytes 4096 | tf_op jit(solution)/shard_map/psum | solution.py:66
  1113.1 9.4 all-gather.3.cloned.1.call-done
  1122.6 3.5 fusion.28
  1126.1 22.9 %all-to-all-start.1 = ((bf16[8,20,96]{2,1,0:T(8,128)(2,1)}), bf16[8,20,96]{2,1,0:T(8,128)(2,1)S(1)}, u32[]{:S(2)}, u32[]{:S(2)}) async-start(bf16[8,20,96]{2,1,0:T(8,128)(2,1)} %fusion.28), calls=%async_computation.2 | async-start | bytes 98304 | tf_op jit(solution)/shard_map/all_to_all | solution.py:97
  1149.0 0.1 copy.46
  1149.1 4.7 all-to-all-done.1
  1153.8 0.7 gather_fusion
  1154.5 0.2 multiply_reduce_fusion
  1154.7 0.6 add_convert_fusion
  (31 shorter events, 0.2 us)
Async XLA Ops:
  6.5 989.9 %copy-start = (bf16[1,6144,128]{2,1,0:T(8,128)(2,1)S(1)}, bf16[1,6144,128]{2,1,0:T(8,128)(2,1)}, u32[]{:S(2)}) copy-start(bf16[1,6144,128]{2,1,0:T(8,128)(2,1)} %param.25) | copy-start | bytes 4718596
  6.5 654.0 %all-reduce.2.cloned.1.call-start = ((), (), s32[]{:S(2)}) async-start(), calls=%async_computation.3 | async-start | bytes 3145728 | tf_op jit(solution)/shard_map/psum | solution.py:52
  91.6 226.1 %copy-start.16 = (bf16[512,128]{1,0:T(8,128)(2,1)S(1)}, bf16[512,128]{1,0:T(8,128)(2,1)}, u32[]{:S(2)}) copy-start(bf16[512,128]{1,0:T(8,128)(2,1)} %param.17) | copy-start | bytes 393220
  323.4 387.8 %reduce-scatter.2.cloned.1.call-start = ((), (), s32[]{:S(2)}) async-start(), calls=%async_computation.4 | async-start | bytes 294912 | tf_op jit(solution)/shard_map/reduce_scatter | solution.py:55
  327.6 335.1 %copy-start.4 = (bf16[768,96]{0,1:T(8,128)(2,1)S(1)}, bf16[768,96]{0,1:T(8,128)(2,1)}, u32[]{:S(2)}) copy-start(bf16[768,96]{0,1:T(8,128)(2,1)} %param.20) | copy-start | bytes 442372
  327.6 336.3 %copy-start.8 = (s32[64,2]{0,1:T(2,128)S(1)}, s32[64,2]{0,1:T(2,128)}, u32[]{:S(2)}) copy-start(s32[64,2]{0,1:T(2,128)} %param.23) | copy-start | bytes 1540
  327.6 336.3 %copy-start.11 = (s32[64,2]{0,1:T(2,128)S(1)}, s32[64,2]{0,1:T(2,128)}, u32[]{:S(2)}) copy-start(s32[64,2]{0,1:T(2,128)} %param.24) | copy-start | bytes 1540
  327.6 383.6 %copy-start.5 = (bf16[64,96]{1,0:T(8,128)(2,1)S(1)}, bf16[64,96]{1,0:T(8,128)(2,1)}, u32[]{:S(2)}) copy-start(bf16[64,96]{1,0:T(8,128)(2,1)} %param.14) | copy-start | bytes 36868
  327.6 500.0 %copy-start.12 = (f32[96]{0:T(128)S(1)}, f32[96]{0:T(128)}, u32[]{:S(2)}) copy-start(f32[96]{0:T(128)} %param.21) | copy-start | bytes 1156
  663.8 458.7 %all-gather.3.cloned.1.call-start = ((), (), s32[]{:S(2)}) async-start(), calls=%async_computation.5 | async-start | bytes 3194880 | tf_op jit(solution)/shard_map/all_gather | solution.py:93
  664.5 0.6 copy-start.6
  827.7 73.8 %copy-start.14 = (f32[64]{0:T(128)}, f32[64]{0:T(128)S(1)}, u32[]{:S(2)}) copy-start(f32[64]{0:T(128)S(1)} %add_rsqrt_fusion) | copy-start | bytes 772
  996.4 1.4 copy-start.1
  996.4 2.8 copy-start.7
  996.4 3.1 copy-start.10
  996.4 3.2 copy-start.3
  996.4 3.2 copy-start.13
  996.5 3.2 copy-start.15
  996.5 3.2 copy-start.17
  997.8 115.3 %copy-start.9 = (s32[64,2]{0,1:T(2,128)S(1)}, s32[64,2]{0,1:T(2,128)}, u32[]{:S(2)}) copy-start(s32[64,2]{0,1:T(2,128)} %param.23) | copy-start | bytes 1540
  997.8 124.7 %copy-start.2 = (bf16[1,8192,96]{1,2,0:T(8,128)(2,1)S(1)}, bf16[1,8192,96]{1,2,0:T(8,128)(2,1)}, u32[]{:S(2)}) copy-start(bf16[1,8192,96]{1,2,0:T(8,128)(2,1)} %param.27) | copy-start | bytes 4718596
  1126.1 27.7 %all-to-all-start.1 = ((bf16[8,20,96]{2,1,0:T(8,128)(2,1)}), bf16[8,20,96]{2,1,0:T(8,128)(2,1)S(1)}, u32[]{:S(2)}, u32[]{:S(2)}) async-start(bf16[8,20,96]{2,1,0:T(8,128)(2,1)} %fusion.28), calls=%async_computation.2 | async-start | bytes 98304 | tf_op jit(solution)/shard_map/all_to_all | solution.py:97
Sparse Core Ops, SparseCore 0:
  323.6 336.9 all-reduce.1
  664.0 47.1 reduce-scatter.1
  999.4 123.1 all-gather.2
where the time goes:
time: 1160 us
  blocking collectives  914 us (79%)
  waiting for transfers between devices  173 us (15%)
  starting transfers between devices  23 us (2%)
  matrix products  19.2 us (2%)
  between operations  13.4 us (1%)
  other arithmetic  11.6 us (1%)
    pmax x1, blocking collectives, per_device(): peak = lax.pmax(local_peak, 'ctx')  221 us
    psum x1, blocking collectives, per_device(): numerator, denominator = lax.psum((numerator, denominator), 'ctx')  220 us
    psum x1, blocking collectives, per_device(): squares = lax.psum(jnp.sum(residual * residual, axis=1), 'ctx')  116 us
    psum x1, blocking collectives, per_device(): lax.psum(jnp.dot(scaled * inverse[:, None], router_wide, precision=lax.Pr...  113 us
    psum x1, waiting for transfers between devices, per_device(): numerator, denominator = lax.psum((numerator, denominator), 'ctx')  113 us
    all_to_all x1, blocking collectives, per_device(): lax.all_to_all(outgoing, 'exp', split_axis=0, concat_axis=0, tiled=True)  88.6 us
    all_gather x1, blocking collectives, per_device(): all_queries = lax.all_gather(queries, 'ctx', axis=0, tiled=True)  82.7 us
    all_gather x1, blocking collectives, per_device(): feature_rows = lax.all_gather(normed, 'ctx', axis=1, tiled=True)  72.3 us
  transfers between devices with their start and end apart: 4, of which 4 were waited for; matrix products, arithmetic and copies ran while one was open for 1% of the time, Pallas kernels for 0%

commit v1 on v0

--- a/solution.py
+++ b/solution.py
@@ -27,7 +27,9 @@
     w_up,
     w_down,
 ):
-    all_queries = lax.all_gather(queries, "ctx", axis=0, tiled=True)
+    all_queries = jnp.concatenate(
+        lax.all_to_all(jnp.stack([queries] * lax.axis_size("ctx")), "ctx", 0, 0), axis=0
+    )
     token_count = all_queries.shape[0]
     cache_length = keys.shape[0]
     groups_local = keys.shape[1] // HD

time: 1160 us -> 1120 us (0.966)
  blocking collectives: 914 us -> 831 us
  starting transfers between devices: 23 us -> 42.3 us
  waiting for transfers between devices: 173 us -> 187 us
    all_gather x1 -> x0, blocking collectives: 82.7 us -> none  [per_device(): all_queries = lax.all_gather(queries, 'ctx', axis=0, tiled=True)]
    all_to_all x0 -> x1, waiting for transfers between devices: none -> 37.9 us  [per_device(): lax.all_to_all(jnp.stack([queries] * lax.axis_size('ctx')), 'ctx', 0, 0)]
    psum x1, waiting for transfers between devices: 113 us -> 89.1 us  [per_device(): numerator, denominator = lax.psum((numerator, denominator), 'ctx')]
    all_to_all x0 -> x1, starting transfers between devices: none -> 19.3 us  [per_device(): lax.all_to_all(jnp.stack([queries] * lax.axis_size('ctx')), 'ctx', 0, 0)]
  transfers between devices with their start and end apart: 4 -> 5, of which waited for: 4 -> 5; matrix products, arithmetic and copies ran while one was open for 1% -> 1% of each run, Pallas kernels for 0% -> 0%
where the time goes in v1:
time: 1120 us; the launch traced here: 1110 us
  blocking collectives  831 us (74%)
  waiting for transfers between devices  187 us (17%)
  starting transfers between devices  42.3 us (4%)
  matrix products  18.3 us (2%)
  between operations  13.4 us (1%)
  other arithmetic  11.5 us (1%)
    pmax x1, blocking collectives, per_device(): peak = lax.pmax(local_peak, 'ctx')  222 us
    psum x1, blocking collectives, per_device(): numerator, denominator = lax.psum((numerator, denominator), 'ctx')  219 us
    psum x1, blocking collectives, per_device(): squares = lax.psum(jnp.sum(residual * residual, axis=1), 'ctx')  116 us
    psum x1, blocking collectives, per_device(): lax.psum(jnp.dot(scaled * inverse[:, None], router_wide, precision=lax.Pr...  113 us
    psum x1, waiting for transfers between devices, per_device(): numerator, denominator = lax.psum((numerator, denominator), 'ctx')  89.1 us
    all_to_all x1, blocking collectives, per_device(): lax.all_to_all(outgoing, 'exp', split_axis=0, concat_axis=0, tiled=True)  88.5 us
    all_gather x1, blocking collectives, per_device(): feature_rows = lax.all_gather(normed, 'ctx', axis=1, tiled=True)  72.4 us
    reduce_scatter x1, waiting for transfers between devices, per_device(): lax.psum_scatter(jnp.dot(attention, out_weight, preferred_element_type=jn...  45.7 us
  transfers between devices with their start and end apart: 5, of which 5 were waited for; matrix products, arithmetic and copies ran while one was open for 1% of the time, Pallas kernels for 0%

profile of v1, /device:TPU:1, one launch (start us, length us, event | category | flops | bytes accessed | tf_op | source)
XLA Modules:
  0.0 1114.2 jit_solution(7173744732596743457)
XLA Ops:
  6.5 0.0 copy-start
  6.5 1.8 stack.2
  8.3 19.3 %all-to-all-start = ((bf16[64,8,768]{2,1,0:T(8,128)(2,1)}), bf16[64,8,768]{2,1,0:T(8,128)(2,1)S(1)}, u32[]{:S(2)}, u32[]{:S(2)}) async-start(bf16[64,8,768]{2,1,0:T(8,128)(2,1)} %stack.2), calls=%async_computation | async-start | bytes 1572864 | tf_op jit(solution)/shard_map/all_to_all | solution.py:31
  27.6 0.0 all-reduce.2.cloned.1.call-start
  27.7 0.7 compare_reduce_fusion.1
  28.4 0.9 compare_reduce_fusion
  29.3 0.1 copy.39
  29.4 0.1 broadcast_bitcast_fusion
  29.5 37.9 %all-to-all-done = bf16[64,8,768]{2,1,0:T(8,128)(2,1)S(1)} async-done(((bf16[64,8,768]{2,1,0:T(8,128)(2,1)}), bf16[64,8,768]{2,1,0:T(8,128)(2,1)S(1)}, u32[]{:S(2)}, u32[]{:S(2)}) %all-to-all-start) | async-done | bytes 786464 | tf_op jit(solution)/shard_map/all_to_all | solution.py:31
  67.4 0.9 reshape.87
  68.3 0.1 broadcast_in_dim.67
  68.4 0.0 copy-start.17
  68.4 3.9 fusion
  72.3 222.5 %pmax.7 = f32[512,6]{0,1:T(8,128)S(1)} all-reduce(f32[512,6]{0,1:T(8,128)S(1)} %get-tuple-element.7), channel_id=1, replica_groups=mesh['ctx'=64,'exp'=8] {'ctx'}, use_global_device_ids=true, to_apply=%region_3.4 | all-reduce | flops 3072 | bytes 24576 | tf_op jit(solution)/shard_map/pmax | solution.py:50
  294.7 5.6 fusion.13
  300.4 0.0 all-reduce.2.cloned.1.call-update
  300.4 0.0 reduce-scatter.2.cloned.1.call-start
  300.5 4.1 convert_reduce_fusion
  304.5 0.0 copy-start.4
  304.6 0.0 copy-start.9
  304.6 0.0 copy-start.12
  304.6 0.0 copy-start.5
  304.6 0.0 copy-start.13
  304.6 219.0 %psum.29 = f32[512,6]{0,1:T(8,128)S(1)} all-reduce(f32[512,6]{0,1:T(8,128)S(1)} %convert_reduce_fusion), channel_id=1, replica_groups=mesh['ctx'=64,'exp'=8] {'ctx'}, use_global_device_ids=true, to_apply=%region_6.7 | all-reduce | flops 3072 | bytes 24576 | tf_op jit(solution)/shard_map/psum | solution.py:54
  523.6 89.1 %all-reduce.2.cloned.1.call-done = f32[512,1,6,128]{3,0,2,1:T(8,128)} async-done(((f32[512,1,6,128]{3,0,2,1:T(8,128)}), f32[512,1,6,128]{3,0,2,1:T(8,128)}) %all-reduce.2.cloned.1.call-update) | async-done | bytes 1572880 | tf_op jit(solution)/shard_map/psum | solution.py:54
  612.8 1.9 divide_convert_fusion
  614.6 0.3 copy.42
  614.9 1.1 fusion.45
  616.0 0.0 reduce-scatter.2.cloned.1.call-update
  616.1 0.0 all-gather.3.cloned.1.call-start
  616.1 0.0 copy-done.9
  616.1 0.0 copy-done.12
  616.1 0.6 compare_and_fusion
  616.7 0.6 copy-done.7
  617.3 0.7 fusion.38
  618.0 45.7 %reduce-scatter.2.cloned.1.call-done = f32[64,96]{1,0:T(8,128)} async-done(((f32[512,96]{1,0:T(8,128)}), f32[64,96]{1,0:T(8,128)}) %reduce-scatter.2.cloned.1.call-update) | async-done | bytes 24592 | tf_op jit(solution)/shard_map/reduce_scatter | solution.py:57
  663.6 0.9 multiply_reduce_fusion.1
  664.5 115.6 %psum.30 = f32[64]{0:T(128)S(1)} all-reduce(f32[64]{0:T(128)S(1)} %multiply_reduce_fusion.1), channel_id=1, replica_groups=mesh['ctx'=64,'exp'=8] {'ctx'}, use_global_device_ids=true, to_apply=%region_9.10 | all-reduce | flops 64 | bytes 512 | tf_op jit(solution)/shard_map/psum | solution.py:66
  780.1 0.8 fusion.41
  780.9 72.4 %all-gather = bf16[64,96,64]{1,2,0:T(8,128)(2,1)S(1)} all-gather(bf16[1,96,64]{1,2,0:T(8,128)(2,1)S(1)} %fusion.41), channel_id=1, replica_groups=mesh['ctx'=64,'exp'=8] {'ctx'}, dimensions={0}, use_global_device_ids=true | all-gather | bytes 798720 | tf_op jit(solution)/shard_map/all_gather | solution.py:82
  853.3 0.7 copy.45
  854.0 2.3 reshape.109
  856.3 1.8 convolution_convert_fusion
  858.2 2.1 reshape.90
  860.3 88.5 %all_to_all.15 = bf16[8,20,6144]{2,1,0:T(8,128)(2,1)S(1)} all-to-all(bf16[8,20,6144]{2,1,0:T(8,128)(2,1)} %reshape.90), channel_id=1, replica_groups=mesh['ctx'=64,'exp'=8] {'exp'}, dimensions={0} | all-to-all | bytes 3932160 | tf_op jit(solution)/shard_map/all_to_all | solution.py:87
  948.8 0.0 copy-start.14
  948.8 0.0 copy-start.18
  948.8 0.8 fusion.16
  949.6 0.6 copy-done.1
  950.2 1.4 fusion.25
  951.6 0.0 all-gather.3.cloned.1.call-update
  951.6 0.1 copy.46
  951.7 0.1 reshape.100
  951.9 0.1 copy.44
  952.0 0.2 fusion.40
  952.2 113.2 %psum.31 = f32[64,8]{0,1:T(8,128)S(1)} all-reduce(f32[64,8]{0,1:T(8,128)S(1)} %fusion.40), channel_id=1, replica_groups=mesh['ctx'=64,'exp'=8] {'ctx'}, use_global_device_ids=true, to_apply=%region_10.11 | all-reduce | flops 512 | bytes 4096 | tf_op jit(solution)/shard_map/psum | solution.py:68
  1065.5 9.4 all-gather.3.cloned.1.call-done
  1074.9 3.5 fusion.28
  1078.4 22.9 %all-to-all-start.2 = ((bf16[8,20,96]{2,1,0:T(8,128)(2,1)}), bf16[8,20,96]{2,1,0:T(8,128)(2,1)S(1)}, u32[]{:S(2)}, u32[]{:S(2)}) async-start(bf16[8,20,96]{2,1,0:T(8,128)(2,1)} %fusion.28), calls=%async_computation.3 | async-start | bytes 98304 | tf_op jit(solution)/shard_map/all_to_all | solution.py:99
  1101.3 0.1 copy.43
  1101.4 4.7 all-to-all-done.2
  1106.2 0.7 gather_fusion
  1106.9 0.2 multiply_reduce_fusion
  1107.1 0.6 add_convert_fusion
  (35 shorter events, 0.2 us)
Async XLA Ops:
  6.5 942.2 %copy-start = (bf16[1,6144,128]{2,1,0:T(8,128)(2,1)S(1)}, bf16[1,6144,128]{2,1,0:T(8,128)(2,1)}, u32[]{:S(2)}) copy-start(bf16[1,6144,128]{2,1,0:T(8,128)(2,1)} %param.25) | copy-start | bytes 4718596
  6.5 61.8 %copy-start.6 = (bf16[512,128]{1,0:T(8,128)(2,1)S(1)}, bf16[512,128]{1,0:T(8,128)(2,1)}, u32[]{:S(2)}) copy-start(bf16[512,128]{1,0:T(8,128)(2,1)} %param.16) | copy-start | bytes 393220
  8.3 59.1 %all-to-all-start = ((bf16[64,8,768]{2,1,0:T(8,128)(2,1)}), bf16[64,8,768]{2,1,0:T(8,128)(2,1)S(1)}, u32[]{:S(2)}, u32[]{:S(2)}) async-start(bf16[64,8,768]{2,1,0:T(8,128)(2,1)} %stack.2), calls=%async_computation | async-start | bytes 1572864 | tf_op jit(solution)/shard_map/all_to_all | solution.py:31
  27.6 585.2 %all-reduce.2.cloned.1.call-start = ((), (), s32[]{:S(2)}) async-start(), calls=%async_computation.4 | async-start | bytes 3145728 | tf_op jit(solution)/shard_map/psum | solution.py:54
  68.4 226.4 %copy-start.17 = (bf16[512,128]{1,0:T(8,128)(2,1)S(1)}, bf16[512,128]{1,0:T(8,128)(2,1)}, u32[]{:S(2)}) copy-start(bf16[512,128]{1,0:T(8,128)(2,1)} %param.17) | copy-start | bytes 393220
  300.4 363.2 %reduce-scatter.2.cloned.1.call-start = ((), (), s32[]{:S(2)}) async-start(), calls=%async_computation.5 | async-start | bytes 294912 | tf_op jit(solution)/shard_map/reduce_scatter | solution.py:57
  304.5 310.4 %copy-start.4 = (bf16[768,96]{0,1:T(8,128)(2,1)S(1)}, bf16[768,96]{0,1:T(8,128)(2,1)}, u32[]{:S(2)}) copy-start(bf16[768,96]{0,1:T(8,128)(2,1)} %param.20) | copy-start | bytes 442372
  304.6 311.6 %copy-start.9 = (s32[64,2]{0,1:T(2,128)S(1)}, s32[64,2]{0,1:T(2,128)}, u32[]{:S(2)}) copy-start(s32[64,2]{0,1:T(2,128)} %param.23) | copy-start | bytes 1540
  304.6 311.6 %copy-start.12 = (s32[64,2]{0,1:T(2,128)S(1)}, s32[64,2]{0,1:T(2,128)}, u32[]{:S(2)}) copy-start(s32[64,2]{0,1:T(2,128)} %param.24) | copy-start | bytes 1540
  304.6 359.0 %copy-start.5 = (bf16[64,96]{1,0:T(8,128)(2,1)S(1)}, bf16[64,96]{1,0:T(8,128)(2,1)}, u32[]{:S(2)}) copy-start(bf16[64,96]{1,0:T(8,128)(2,1)} %param.14) | copy-start | bytes 36868
  304.6 475.5 %copy-start.13 = (f32[96]{0:T(128)S(1)}, f32[96]{0:T(128)}, u32[]{:S(2)}) copy-start(f32[96]{0:T(128)} %param.21) | copy-start | bytes 1156
  616.1 458.9 %all-gather.3.cloned.1.call-start = ((), (), s32[]{:S(2)}) async-start(), calls=%async_computation.6 | async-start | bytes 3194880 | tf_op jit(solution)/shard_map/all_gather | solution.py:95
  616.7 0.6 copy-start.7
  780.1 73.9 %copy-start.15 = (f32[64]{0:T(128)}, f32[64]{0:T(128)S(1)}, u32[]{:S(2)}) copy-start(f32[64]{0:T(128)S(1)} %add_rsqrt_fusion) | copy-start | bytes 772
  948.8 1.4 copy-start.1
  948.8 2.8 copy-start.8
  948.8 3.1 copy-start.11
  948.8 3.2 copy-start.3
  948.8 3.2 copy-start.14
  948.8 3.2 copy-start.16
  948.8 3.2 copy-start.18
  950.2 115.3 %copy-start.10 = (s32[64,2]{0,1:T(2,128)S(1)}, s32[64,2]{0,1:T(2,128)}, u32[]{:S(2)}) copy-start(s32[64,2]{0,1:T(2,128)} %param.23) | copy-start | bytes 1540
  950.2 124.7 %copy-start.2 = (bf16[1,8192,96]{1,2,0:T(8,128)(2,1)S(1)}, bf16[1,8192,96]{1,2,0:T(8,128)(2,1)}, u32[]{:S(2)}) copy-start(bf16[1,8192,96]{1,2,0:T(8,128)(2,1)} %param.27) | copy-start | bytes 4718596
  1078.4 27.7 %all-to-all-start.2 = ((bf16[8,20,96]{2,1,0:T(8,128)(2,1)}), bf16[8,20,96]{2,1,0:T(8,128)(2,1)S(1)}, u32[]{:S(2)}, u32[]{:S(2)}) async-start(bf16[8,20,96]{2,1,0:T(8,128)(2,1)} %fusion.28), calls=%async_computation.3 | async-start | bytes 98304 | tf_op jit(solution)/shard_map/all_to_all | solution.py:99
Sparse Core Ops, SparseCore 0:
  300.5 312.1 all-reduce.1
  616.2 47.3 reduce-scatter.1
  951.7 123.1 all-gather.2
